TPU v7x, 128 devices: a whole 4x4x4 slice. The times are simulated.
128 devices in a mesh: frame: 4 (over x_hi, core), patch: 32 (over x_lo, y, z).
Axes of the slice: x: 4 (x_hi: 2, x_lo: 2; x = x_hi * 2 + x_lo), y: 4, z: 4, core: 2. Of those that a mesh axis runs over, the one named last changes fastest.
Arguments:
- latent: bfloat16 [4, 64, 192, 640], P('frame', 'patch'), may hold values from -32 to 32
- gn_gain: float32 [640], replicated, may hold values from 0.1 to 1.9
- gn_bias: float32 [640], replicated, may hold values from -3 to 3
- conv_weight: bfloat16 [3, 3, 640, 640], replicated, may hold values from -0.15625 to 0.15625
- w_query: bfloat16 [640, 384], replicated, may hold values from -0.25 to 0.25
- w_kv: bfloat16 [640, 768], replicated, may hold values from -0.25 to 0.25
- w_out: bfloat16 [384, 640], replicated, may hold values from -0.3125 to 0.3125
- stale_kv: bfloat16 [4, 64, 192, 768], P('frame', 'patch'), may hold values from -190 to 190
- ln_gain: float32 [640], replicated, may hold values from 0.5 to 24
- ln_bias: float32 [640], replicated, may hold values from -3 to 3
- t_query: bfloat16 [640, 640], replicated, may hold values from -0.25 to 0.25
- t_kv: bfloat16 [640, 1280], replicated, may hold values from -0.25 to 0.25
- t_out: bfloat16 [640, 640], replicated, may hold values from -0.25 to 0.25
Outputs:
- block_out: float32 [4, 64, 192, 640], P('frame', 'patch')
- fresh_kv: bfloat16 [4, 64, 192, 768], P('frame', 'patch')
All inputs are finite; a program needn't handle non-finite values.
Results may differ from a plain program's by a relative error of at most 0.04.
The roundings to bfloat16 on the way count: a program that leaves them out, or rounds other values in their place, can miss the bound.
Values may be sent and summed in bfloat16 or wider, within the bound.
A program may use at most 384 MiB of HBM per device.

v0:
```python
import math

import jax
import jax.numpy as jnp
from jax import lax
from jax.sharding import PartitionSpec as P

THEADS = 8
GROUPS = 32
HEADS = 6
HEAD = 64
THEAD = 80


def extended(block, sides, width):
    for axis, dim in sides:
        count = lax.axis_size(axis)
        forward = [(i, i + 1) for i in range(count - 1)]
        backward = [(target, source) for source, target in forward]
        low = lax.ppermute(
            lax.slice_in_dim(block, block.shape[dim] - width, None, axis=dim), axis, forward
        )
        high = lax.ppermute(lax.slice_in_dim(block, 0, width, axis=dim), axis, backward)
        block = jnp.concatenate([low, block, high], axis=dim)
    return block


def position_code(frame_pos, channels):
    halves = jnp.arange(channels // 2, dtype=jnp.float32)
    freqs = jnp.exp(-math.log(10000.0) * 2.0 * halves / channels)
    angles = frame_pos[:, None] * freqs[None, :]
    return jnp.stack([jnp.sin(angles), jnp.cos(angles)], axis=-1).reshape(
        frame_pos.shape[0], channels
    )


def head_scores(query_rows, key_rows):
    return lax.dot_general(
        query_rows, key_rows, (((1,), (1,)), ((), ())), preferred_element_type=jnp.float32
    ) * HEAD ** (-0.5)


def frame_attention(q_frames, kv_frames):
    query_frames, count, channels = q_frames.shape
    q_heads = q_frames.reshape(query_frames, count, THEADS, THEAD)
    k_heads = kv_frames[..., :channels].reshape(-1, count, THEADS, THEAD)
    v_heads = kv_frames[..., channels:].reshape(-1, count, THEADS, THEAD)
    tscores = jnp.einsum(
        "fthd,gthd->fthg", q_heads, k_heads, preferred_element_type=jnp.float32
    ) * THEAD ** (-0.5)
    texp = jnp.exp(tscores - jnp.max(tscores, axis=-1, keepdims=True))
    ttotals = jnp.sum(texp, axis=-1)
    tweighted = jnp.einsum(
        "fthg,gthd->fthd", texp.astype(jnp.bfloat16), v_heads, preferred_element_type=jnp.float32
    )
    return (
        (tweighted / ttotals[..., None]).reshape(query_frames, count, channels).astype(jnp.bfloat16)
    )


def shards(
    latent,
    gn_gain,
    gn_bias,
    conv_weight,
    w_query,
    w_kv,
    w_out,
    stale_kv,
    ln_gain,
    ln_bias,
    t_query,
    t_kv,
    t_out,
):
    frames_here, row_count, columns, channels = latent.shape
    per_group = channels // GROUPS
    tokens_here = frames_here * row_count * columns
    inner = HEADS * HEAD
    my_patch = lax.axis_index("patch")
    zero_index = jnp.zeros((), jnp.int32)
    own_start = my_patch * tokens_here
    wide = latent.astype(jnp.float32).reshape(frames_here, row_count * columns, GROUPS, per_group)
    sum_one = jnp.sum(wide, axis=(1, 3))
    sum_two = jnp.sum(wide * wide, axis=(1, 3))
    total_one, total_two = lax.psum((sum_one, sum_two), "patch")
    count = row_count * lax.axis_size("patch") * columns * per_group
    center = total_one / count
    variance = total_two / count - center * center
    normed = (wide - center[:, None, :, None]) * lax.rsqrt(variance + 1e-05)[:, None, :, None]
    activ = normed.reshape(frames_here, row_count, columns, channels) * gn_gain + gn_bias
    hidden = jax.nn.silu(activ).astype(jnp.bfloat16)
    padded = extended(hidden, (("patch", 1),), 1)
    conv = lax.conv_general_dilated(
        padded,
        conv_weight,
        (1, 1),
        ((0, 0), (1, 1)),
        dimension_numbers=("NHWC", "HWIO", "NHWC"),
        preferred_element_type=jnp.float32,
    )
    resid = (latent.astype(jnp.float32) + conv).astype(jnp.bfloat16).reshape(tokens_here, channels)
    query = jnp.dot(resid, w_query, preferred_element_type=jnp.float32).astype(jnp.bfloat16)
    fresh = jnp.dot(resid, w_kv, preferred_element_type=jnp.float32).astype(jnp.bfloat16)
    gathered = lax.all_gather(stale_kv, "patch", axis=1, tiled=True).reshape(-1, 2 * inner)
    keys_vals = lax.dynamic_update_slice(gathered, fresh, (own_start, zero_index))
    pieces = []
    for head_index in range(HEADS):
        low = head_index * HEAD
        scores = head_scores(query[:, low : low + HEAD], keys_vals[:, low : low + HEAD])
        shifted = jnp.exp(scores - jnp.max(scores, axis=1, keepdims=True))
        totals = jnp.sum(shifted, axis=1, keepdims=True)
        weighted = jnp.dot(
            shifted.astype(jnp.bfloat16),
            keys_vals[:, inner + low : inner + low + HEAD],
            preferred_element_type=jnp.float32,
        )
        pieces.append(weighted / totals)
    attn = jnp.concatenate(pieces, axis=1).astype(jnp.bfloat16)
    mixed = (
        resid.astype(jnp.float32) + jnp.dot(attn, w_out, preferred_element_type=jnp.float32)
    ).astype(jnp.bfloat16)
    mixed_wide = mixed.astype(jnp.float32)
    lcenter = jnp.mean(mixed_wide, axis=-1, keepdims=True)
    lvar = jnp.mean(jnp.square(mixed_wide - lcenter), axis=-1, keepdims=True)
    frame_pos = (lax.axis_index("frame") * frames_here + jnp.arange(frames_here)).astype(
        jnp.float32
    )
    codes = position_code(frame_pos, channels)
    units = (
        (mixed_wide - lcenter) * lax.rsqrt(lvar + 1e-05) * ln_gain + ln_bias + codes[0][None, :]
    ).astype(jnp.bfloat16)
    t_q = jnp.dot(units, t_query, preferred_element_type=jnp.float32).astype(jnp.bfloat16)
    t_k = jnp.dot(units, t_kv, preferred_element_type=jnp.float32).astype(jnp.bfloat16)
    kv_frames = lax.all_gather(t_k[None], "frame", axis=0, tiled=True)
    tattn = frame_attention(t_q[None], kv_frames)[0]
    final = mixed_wide + jnp.dot(tattn, t_out, preferred_element_type=jnp.float32)
    return (
        final.reshape(frames_here, row_count, columns, channels),
        fresh.reshape(frames_here, row_count, columns, 2 * inner),
    )


def solution(mesh):
    placed = (
        P("frame", "patch", None, None),
        P(),
        P(),
        P(),
        P(),
        P(),
        P(),
        P("frame", "patch", None, None),
        P(),
        P(),
        P(),
        P(),
        P(),
    )
    return jax.shard_map(
        shards,
        mesh=mesh,
        in_specs=placed,
        out_specs=(P("frame", "patch", None, None), P("frame", "patch", None, None)),
        check_vma=False,
    )
```

profile of v0, /device:TPU:1, one launch (start us, length us, event | category | flops | bytes accessed | tf_op | source)
XLA Modules:
  0.0 472.3 jit_solution(11955192771459171868)
XLA Ops:
  9.6 76.2 %all-reduce = (f32[1,32]{1,0:T(1,128)S(1)}, f32[1,32]{1,0:T(1,128)S(1)}) all-reduce(f32[1,32]{1,0:T(1,128)S(1)} %bitcast.56, f32[1,32]{1,0:T(1,128)S(1)} %bitcast.57), channel_id=1, replica_groups=mesh['frame'=4,'patch'=32] {'patch'}, use_global_device_ids=true, to_apply=%region_5.6 | all-reduce | flops 64 | bytes 512 | tf_op jit(solution)/shard_map/psum | solution.py:86
  89.7 4.7 collective-permute-start
  94.8 6.4 %collective-permute-done.1 = bf16[1,1,192,640]{3,2,1,0:T(8,128)(2,1)S(1)} collective-permute-done((bf16[1,1,192,640]{3,2,1,0:T(8,128)(2,1)}, bf16[1,1,192,640]{3,2,1,0:T(8,128)(2,1)S(1)}, u32[]{:S(2)}, u32[]{:S(2)}) %collective-permute-start.1) | collective-permute-done | bytes 245792 | tf_op jit(solution)/shard_map/ppermute | solution.py:23
  104.4 7.0 %convolution_select_fusion = f32[2,8,25,640]{3,1,2,0:T(8,128)S(1)} fusion(bf16[3,3,640,640]{3,2,1,0:T(8,128)(2,1)} %param.16, bf16[4,1,7,2,640]{4,2,3,0,1:T(8,128)(2,1)S(1)} %slice.92, bf16[4,1,8,25,640]{4,2,3,0,1:T(8,128)(2,1)S(1)} %copy.45, pred[8,25]{0,1:T(8,128)(4,1)} %constant.49), kind=kOutput, calls=%fused_computation.62 | convolution fusion | flops 2952693760 | bytes 9492680 | tf_op jit(solution)/shard_map/conv_general_dilated | solution.py:94
  113.0 115.5 %all-gather.4.cloned.1.call-done = bf16[1,64,192,768]{3,2,0,1:T(8,128)(2,1)} async-done(((bf16[1,2,192,768]{3,2,0,1:T(8,128)(2,1)}), bf16[1,64,192,768]{3,2,0,1:T(8,128)(2,1)}) %all-gather.4.cloned.1.call-update) | async-done | bytes 18874384 | tf_op jit(solution)/shard_map/all_gather | solution.py:105
  228.4 2.9 constant_dynamic-update-slice_fusion
  231.3 12.9 %fusion.177 = (f32[384]{0:T(512)S(1)}, f32[384,12288]{1,0:T(8,128)}) fusion(bf16[12288,768]{1,0:T(8,128)(2,1)} %get-tuple-element.14, bf16[384,384]{0,1:T(8,128)(2,1)S(1)} %convolution_convert_fusion.3), kind=kOutput, calls=%fused_computation.136 | convolution fusion | flops 613416576 | bytes 22070784 | tf_op jit(solution)/shard_map/dot_general | solution.py:38
  244.2 8.2 %fusion.178 = (f32[384]{0:T(512)S(1)}, f32[384,12288]{1,0:T(8,128)}) fusion(bf16[12288,768]{1,0:T(8,128)(2,1)S(1)} %copy-done.1, bf16[384,384]{0,1:T(8,128)(2,1)S(1)} %convolution_convert_fusion.3), kind=kOutput, calls=%fused_computation.137 | convolution fusion | flops 613416576 | bytes 22070784 | tf_op jit(solution)/shard_map/dot_general | solution.py:38
  252.4 7.8 %fusion.179 = (f32[384]{0:T(512)S(1)}, f32[384,12288]{1,0:T(8,128)}) fusion(bf16[12288,768]{1,0:T(8,128)(2,1)S(1)} %copy-done.1, bf16[384,384]{0,1:T(8,128)(2,1)S(1)} %convolution_convert_fusion.3), kind=kOutput, calls=%fused_computation.138 | convolution fusion | flops 613416576 | bytes 22070784 | tf_op jit(solution)/shard_map/dot_general | solution.py:38
  260.2 8.0 %fusion.180 = (f32[384]{0:T(512)S(1)}, f32[384,12288]{1,0:T(8,128)}) fusion(bf16[12288,768]{1,0:T(8,128)(2,1)S(1)} %copy-done.1, bf16[384,384]{0,1:T(8,128)(2,1)S(1)} %convolution_convert_fusion.3), kind=kOutput, calls=%fused_computation.139 | convolution fusion | flops 613416576 | bytes 22070784 | tf_op jit(solution)/shard_map/dot_general | solution.py:38
  268.2 7.8 %fusion.181 = (f32[384]{0:T(512)S(1)}, f32[384,12288]{1,0:T(8,128)}) fusion(bf16[12288,768]{1,0:T(8,128)(2,1)S(1)} %copy-done.1, bf16[384,384]{0,1:T(8,128)(2,1)S(1)} %convolution_convert_fusion.3), kind=kOutput, calls=%fused_computation.140 | convolution fusion | flops 613416576 | bytes 22070784 | tf_op jit(solution)/shard_map/dot_general | solution.py:38
  276.0 8.4 %fusion.182 = (f32[384]{0:T(512)S(1)}, f32[384,12288]{1,0:T(8,128)}) fusion(bf16[12288,768]{1,0:T(8,128)(2,1)S(1)} %copy-done.1, bf16[384,384]{0,1:T(8,128)(2,1)S(1)} %convolution_convert_fusion.3), kind=kOutput, calls=%fused_computation.141 | convolution fusion | flops 613416576 | bytes 22070784 | tf_op jit(solution)/shard_map/dot_general | solution.py:38
  284.4 9.0 %fusion = f32[384]{0:T(512)S(1)} fusion(f32[384,12288]{1,0:T(8,128)} %get-tuple-element.17, f32[384]{0:T(512)S(1)} %get-tuple-element.16), kind=kLoop, calls=%fused_computation.12 | loop fusion | flops 9436800 | bytes 18877440 | tf_op jit(solution)/shard_map/reduce_sum | solution.py:112
  293.4 10.2 %fusion.62 = bf16[384,384]{0,1:T(8,128)(2,1)S(1)} fusion(bf16[12288,768]{1,0:T(8,128)(2,1)} %get-tuple-element.14, f32[384,12288]{1,0:T(8,128)} %get-tuple-element.17, f32[384]{0:T(512)S(1)} %get-tuple-element.16, f32[384]{0:T(512)S(1)} %fusion), kind=kOutput, calls=%fused_computation.75 | convolution fusion | flops 613466112 | bytes 22072320 | tf_op jit(solution)/shard_map/dot_general | solution.py:113
  303.6 9.0 %fusion.2 = f32[384]{0:T(512)S(1)} fusion(f32[384,12288]{1,0:T(8,128)} %get-tuple-element.19, f32[384]{0:T(512)S(1)} %get-tuple-element.18), kind=kLoop, calls=%fused_computation.14 | loop fusion | flops 9436800 | bytes 18877440 | tf_op jit(solution)/shard_map/reduce_sum | solution.py:112
  312.6 11.3 %fusion.77 = bf16[384,384]{0,1:T(8,128)(2,1)S(1)} fusion(bf16[384,384]{0,1:T(8,128)(2,1)S(1)} %fusion.62, bf16[12288,768]{1,0:T(8,128)(2,1)} %get-tuple-element.14, f32[384,12288]{1,0:T(8,128)} %get-tuple-element.19, f32[384]{0:T(512)S(1)} %get-tuple-element.18, f32[384]{0:T(512)S(1)} %fusion.2), kind=kOutput, calls=%fused_computation.78 | convolution fusion | flops 613466112 | bytes 22073344 | tf_op jit(solution)/shard_map/dot_general | solution.py:113
  323.9 9.2 %fusion.4 = f32[384]{0:T(512)S(1)} fusion(f32[384,12288]{1,0:T(8,128)} %get-tuple-element.21, f32[384]{0:T(512)S(1)} %get-tuple-element.20), kind=kLoop, calls=%fused_computation.16 | loop fusion | flops 9436800 | bytes 18877440 | tf_op jit(solution)/shard_map/reduce_sum | solution.py:112
  333.1 10.2 %fusion.92 = bf16[384,384]{0,1:T(8,128)(2,1)S(1)} fusion(bf16[384,384]{0,1:T(8,128)(2,1)S(1)} %fusion.77, bf16[12288,768]{1,0:T(8,128)(2,1)} %get-tuple-element.14, f32[384,12288]{1,0:T(8,128)} %get-tuple-element.21, f32[384]{0:T(512)S(1)} %get-tuple-element.20, f32[384]{0:T(512)S(1)} %fusion.4), kind=kOutput, calls=%fused_computation.81 | convolution fusion | flops 613466112 | bytes 22073344 | tf_op jit(solution)/shard_map/dot_general | solution.py:113
  343.3 9.0 %fusion.6 = f32[384]{0:T(512)S(1)} fusion(f32[384,12288]{1,0:T(8,128)} %get-tuple-element.23, f32[384]{0:T(512)S(1)} %get-tuple-element.22), kind=kLoop, calls=%fused_computation.18 | loop fusion | flops 9436800 | bytes 18877440 | tf_op jit(solution)/shard_map/reduce_sum | solution.py:112
  352.3 11.3 %fusion.107 = bf16[384,384]{0,1:T(8,128)(2,1)S(1)} fusion(bf16[384,384]{0,1:T(8,128)(2,1)S(1)} %fusion.92, bf16[12288,768]{1,0:T(8,128)(2,1)} %get-tuple-element.14, f32[384,12288]{1,0:T(8,128)} %get-tuple-element.23, f32[384]{0:T(512)S(1)} %get-tuple-element.22, f32[384]{0:T(512)S(1)} %fusion.6), kind=kOutput, calls=%fused_computation.84 | convolution fusion | flops 613466112 | bytes 22073344 | tf_op jit(solution)/shard_map/dot_general | solution.py:113
  363.7 9.2 %fusion.8 = f32[384]{0:T(512)S(1)} fusion(f32[384,12288]{1,0:T(8,128)} %get-tuple-element.25, f32[384]{0:T(512)S(1)} %get-tuple-element.24), kind=kLoop, calls=%fused_computation.20 | loop fusion | flops 9436800 | bytes 18877440 | tf_op jit(solution)/shard_map/reduce_sum | solution.py:112
  372.9 10.4 %fusion.122 = bf16[384,384]{0,1:T(8,128)(2,1)S(1)} fusion(bf16[384,384]{0,1:T(8,128)(2,1)S(1)} %fusion.107, bf16[12288,768]{1,0:T(8,128)(2,1)} %get-tuple-element.14, f32[384,12288]{1,0:T(8,128)} %get-tuple-element.25, f32[384]{0:T(512)S(1)} %get-tuple-element.24, f32[384]{0:T(512)S(1)} %fusion.8), kind=kOutput, calls=%fused_computation.87 | convolution fusion | flops 613466112 | bytes 22073344 | tf_op jit(solution)/shard_map/dot_general | solution.py:113
  383.2 9.0 %fusion.10 = f32[384]{0:T(512)S(1)} fusion(f32[384,12288]{1,0:T(8,128)} %get-tuple-element.27, f32[384]{0:T(512)S(1)} %get-tuple-element.26), kind=kLoop, calls=%fused_computation.22 | loop fusion | flops 9436800 | bytes 18877440 | tf_op jit(solution)/shard_map/reduce_sum | solution.py:112
  392.2 11.4 %fusion.137 = bf16[384,384]{0,1:T(8,128)(2,1)S(1)} fusion(bf16[384,384]{0,1:T(8,128)(2,1)S(1)} %fusion.122, bf16[12288,768]{1,0:T(8,128)(2,1)} %get-tuple-element.14, f32[384,12288]{1,0:T(8,128)} %get-tuple-element.27, f32[384]{0:T(512)S(1)} %get-tuple-element.26, f32[384]{0:T(512)S(1)} %fusion.10), kind=kOutput, calls=%fused_computation.90 | convolution fusion | flops 613466112 | bytes 22073344 | tf_op jit(solution)/shard_map/dot_general | solution.py:113
  404.9 2.0 convolution_convert_fusion
  410.8 34.7 %all-gather.6.cloned.1.call-done = bf16[1536,1280]{1,0:T(8,128)(2,1)} async-done(((bf16[384,1280]{1,0:T(8,128)(2,1)}), bf16[1536,1280]{1,0:T(8,128)(2,1)}) %all-gather.6.cloned.1.call-update) | async-done | bytes 3932176 | tf_op jit(solution)/shard_map/all_gather | solution.py:135
  445.6 4.5 fusion.175
  450.0 4.0 copy.65
  454.0 4.0 copy.66
  458.1 2.0 multiply_reduce_fusion.1
  460.1 2.1 multiply_reduce_fusion
  462.3 2.7 convert_add_fusion.1
  (55 shorter events, 16.6 us)
Async XLA Ops:
  7.2 397.7 %copy-start = (bf16[640,1280]{1,0:T(8,128)(2,1)S(1)}, bf16[640,1280]{1,0:T(8,128)(2,1)}, u32[]{:S(2)}) copy-start(bf16[640,1280]{1,0:T(8,128)(2,1)} %param.24) | copy-start | bytes 4915204
  7.2 105.2 %copy-start.2 = (bf16[1,2,192,640]{3,2,1,0:T(8,128)(2,1)S(1)}, bf16[1,2,192,640]{3,2,1,0:T(8,128)(2,1)}, u32[]{:S(2)}) copy-start(bf16[1,2,192,640]{3,2,1,0:T(8,128)(2,1)} %param.13) | copy-start | bytes 1474564
  7.2 221.2 %all-gather.4.cloned.1.call-start = ((), (), s32[]{:S(2)}) async-start(), calls=%async_computation | async-start | bytes 19464192 | tf_op jit(solution)/shard_map/all_gather | solution.py:105
  7.9 104.5 %copy-start.3 = (bf16[640,384]{1,0:T(8,128)(2,1)S(1)}, bf16[640,384]{1,0:T(8,128)(2,1)}, u32[]{:S(2)}) copy-start(bf16[640,384]{1,0:T(8,128)(2,1)} %param.17) | copy-start | bytes 1474564
  7.9 437.6 %all-gather.6.cloned.1.call-start = ((), (), s32[]{:S(2)}) async-start(), calls=%async_computation.1 | async-start | bytes 4915200 | tf_op jit(solution)/shard_map/all_gather | solution.py:135
  88.5 12.7 %collective-permute-start.1 = (bf16[1,1,192,640]{3,2,1,0:T(8,128)(2,1)}, bf16[1,1,192,640]{3,2,1,0:T(8,128)(2,1)S(1)}, u32[]{:S(2)}, u32[]{:S(2)}) collective-permute-start(bf16[1,1,192,640]{3,2,1,0:T(8,128)(2,1)} %get-tuple-element.9), channel_id=1, source_target_pairs={{1,0},{2,1},{3,2},{4,3},{5,4},{6,5},{7,6},{8,7},{9,8},{10,9},{11,1... | collective-permute-start | bytes 737288 | tf_op jit(solution)/shard_map/ppermute | solution.py:23
  89.7 12.3 %collective-permute-start = (bf16[1,1,192,640]{3,2,1,0:T(8,128)(2,1)}, bf16[1,1,192,640]{3,2,1,0:T(8,128)(2,1)}, u32[]{:S(2)}, u32[]{:S(2)}) collective-permute-start(bf16[1,1,192,640]{3,2,1,0:T(8,128)(2,1)} %get-tuple-element.8), channel_id=1, source_target_pairs={{0,1},{1,2},{2,3},{3,4},{4,5},{5,6},{6,7},{7,8},{8,9},{9,10},{10,1... | collective-permute-start | bytes 737288 | tf_op jit(solution)/shard_map/ppermute | solution.py:20
  231.3 12.9 %copy-start.1 = (bf16[12288,768]{1,0:T(8,128)(2,1)S(1)}, bf16[12288,768]{1,0:T(8,128)(2,1)}, u32[]{:S(2)}) copy-start(bf16[12288,768]{1,0:T(8,128)(2,1)} %get-tuple-element.14) | copy-start | bytes 56623108
  392.2 11.4 %copy-start.4 = (bf16[384,640]{1,0:T(8,128)(2,1)S(1)}, bf16[384,640]{1,0:T(8,128)(2,1)}, u32[]{:S(2)}) copy-start(bf16[384,640]{1,0:T(8,128)(2,1)} %param.19) | copy-start | bytes 1474564
  392.2 12.6 %copy-start.5 = (f32[640]{0:T(1024)S(1)}, f32[640]{0:T(1024)}, u32[]{:S(2)}) copy-start(f32[640]{0:T(1024)} %param.22) | copy-start | bytes 7684
  392.2 12.6 %copy-start.6 = (f32[640]{0:T(1024)S(1)}, f32[640]{0:T(1024)}, u32[]{:S(2)}) copy-start(f32[640]{0:T(1024)} %param.21) | copy-start | bytes 7684
Sparse Core Ops, SparseCore 0:
  9.7 218.7 all-gather.3
  407.0 38.5 all-gather.5
where the time goes:
time: 481 us; the launch traced here: 472 us
  waiting for transfers between devices  158 us (33%)
  matrix products  136 us (28%)
  blocking collectives  76.2 us (16%)
  other arithmetic  64.1 us (13%)
  local copies, waits for them, and re-layouts  17.3 us (4%)
  between operations  14.8 us (3%)
  starting transfers between devices  6.03 us (1%)
    all_gather x1, waiting for transfers between devices, shards(): lax.all_gather(stale_kv, 'patch', axis=1, tiled=True).reshape(-1, 2 * inner)  115 us
    psum x1, blocking collectives, shards(): total_one, total_two = lax.psum((sum_one, sum_two), 'patch')  76.2 us
    dot_general x6, matrix products, shards(): jnp.dot(shifted.astype(jnp.bfloat16), keys_vals[:, inner + low:inner + lo...  64.9 us
    reduce_sum x6, other arithmetic, shards(): totals = jnp.sum(shifted, axis=1, keepdims=True)  54.3 us
    dot_general x6, matrix products, head_scores(): lax.dot_general(query_rows, key_rows, (((1,), (1,)), ((), ())), preferred...  53.1 us
    all_gather x1, waiting for transfers between devices, shards(): kv_frames = lax.all_gather(t_k[None], 'frame', axis=0, tiled=True)  34.7 us
  transfers between devices with their start and end apart: 4, of which 4 were waited for; matrix products, arithmetic and copies ran while one was open for 4% of the time, Pallas kernels for 0%

commit v1 on v0

v1 whole, which is shorter than its diff:
```python
import math

import jax
import jax.numpy as jnp
import numpy as np
from jax import lax
from jax.experimental import pallas as pl
from jax.experimental.pallas import tpu as pltpu
from jax.sharding import PartitionSpec as P

C = 640
THEADS = 8
GROUPS = 32
HEADS = 6
HEAD = 64
THEAD = 80
HC = 384
W = 192
T = 384
FRAMES = 4
QTR = 96
CHUNK = 1536
BF = jnp.bfloat16
F32 = jnp.float32
SCALE = HEAD ** (-0.5) * math.log2(math.e)
MESH = pl.DeviceIdType.MESH


def kernel(
    lat_h, stale_h, convw_h, wq_h, wkv_h, wout_h, tq_h, tkv_h, tout_h,
    gain_ref, bias_ref, lgain_ref, lbias_ref, code_ref, gmat_h, hsum_ref, hexp_ref,
    out_ref, fresh_h,
    lat, halo, convw, wqkv, wout, wt, tout, gmat, hcat, cacc, resid,
    stat1, stat2, qbuf, kv, acc, lbuf, mbuf, pout, pin, lout, lin,
    units, ubuf, tres, tbuf,
    lsem, hss, hrs, s1s, s1r, s2s, s2r, kss, krs, qss, qrs, pss, prs, lss, lrs, uss, urs, tss, trs,
):
    f = lax.axis_index("frame")
    p = lax.axis_index("patch")
    x = p // 16
    y = (p // 4) % 4
    z = p % 4

    def at(px, py, pz):
        return (f, px * 16 + py * 4 + pz)

    def remote(src, dst, ss, rs, dev):
        return pltpu.make_async_remote_copy(
            src_ref=src, dst_ref=dst, send_sem=ss, recv_sem=rs, device_id=dev, device_id_type=MESH
        )

    xy = [((x + dx) % 2, (y + dy) % 4) for dx, dy in ((0, 1), (0, 3), (1, 0), (0, 2), (1, 1), (1, 3), (1, 2))]
    xy_peers = [at(a, b, z) for a, b in xy]
    z_peers = {s: at(x, y, (z + s) % 4) for s in (1, 2, 3)}
    z_back = {s: at(x, y, (z + 4 - s) % 4) for s in (1, 2, 3)}
    up = (f, (p + 1) % 32)
    down = (f, (p + 31) % 32)
    f_ids = {1: f + 1 - 2 * (f % 2), 2: (f + 2) % 4, 3: 3 - f}
    f_peers = {d: (g, p) for d, g in f_ids.items()}

    loads = [
        pltpu.make_async_copy(lat_h, lat, lsem.at[0]),
        pltpu.make_async_copy(gmat_h, gmat, lsem.at[1]),
        pltpu.make_async_copy(convw_h, convw, lsem.at[2]),
        pltpu.make_async_copy(wq_h, wqkv.at[:, pl.ds(0, HC)], lsem.at[3]),
        pltpu.make_async_copy(wkv_h, wqkv.at[:, pl.ds(HC, 2 * HC)], lsem.at[4]),
        pltpu.make_async_copy(stale_h, kv.at[pl.ds(4 * T, T)], lsem.at[5]),
        pltpu.make_async_copy(wout_h, wout, lsem.at[6]),
        pltpu.make_async_copy(tq_h, wt.at[:, pl.ds(0, C)], lsem.at[7]),
        pltpu.make_async_copy(tkv_h, wt.at[:, pl.ds(C, 2 * C)], lsem.at[8]),
        pltpu.make_async_copy(tout_h, tout, lsem.at[9]),
    ]
    for c in loads:
        c.start()

    barrier = pltpu.get_barrier_semaphore()
    greet = xy_peers + list(z_peers.values()) + [up, down] + list(f_peers.values())
    for dev in greet:
        pl.semaphore_signal(barrier, inc=1, device_id=dev, device_id_type=MESH)

    row8 = lax.broadcasted_iota(jnp.int32, (8, C), 0)
    loads[0].wait()
    wide = lat[...].astype(F32)
    stat1[0, 0:1, :] = jnp.sum(wide, axis=0, keepdims=True)
    stat1[0, 1:2, :] = jnp.sum(wide * wide, axis=0, keepdims=True)
    pl.semaphore_wait(barrier, len(greet))

    sends = []
    st1 = [remote(stat1.at[0], stat1.at[1 + i], s1s.at[i], s1r.at[i], d) for i, d in enumerate(xy_peers)]
    for c in st1:
        c.start()
    halos = [
        remote(lat_h.at[pl.ds(W, W)], halo.at[0], hss.at[0], hrs.at[0], up),
        remote(lat_h.at[pl.ds(0, W)], halo.at[1], hss.at[1], hrs.at[1], down),
    ]
    for c in halos:
        c.start()
    spots = (1, 2, 3, 5)
    kvs = [
        remote(stale_h, kv.at[pl.ds(s * T, T)], kss.at[i], krs.at[i], xy_peers[i])
        for i, s in enumerate(spots)
    ]
    for c in kvs:
        c.start()

    for c in st1:
        c.wait_recv()
    stat2[0] = jnp.sum(stat1[...], axis=0)
    st2 = [remote(stat2.at[0], stat2.at[s], s2s.at[s - 1], s2r.at[s - 1], z_peers[s]) for s in (1, 3, 2)]
    for c in st2:
        c.start()
    loads[1].wait()
    for c in st2:
        c.wait_recv()
    total = jnp.sum(stat2[...], axis=0)
    total8 = jnp.where(row8 == 0, total[0:1], jnp.where(row8 == 1, total[1:2], 0.0))
    hi = total8.astype(BF).astype(F32)
    mid = (total8 - hi).astype(BF).astype(F32)
    low = total8 - hi - mid
    parts = jnp.concatenate([hi, mid, low, jnp.zeros((8, C), F32)], axis=0).astype(BF)
    summed = jnp.dot(parts, gmat[...], preferred_element_type=F32)
    summed = summed[0:8] + summed[8:16] + summed[16:24]
    count = float(32 * T * (C // GROUPS))
    center = summed[0:1] / count
    variance = summed[1:2] / count - center * center
    scale = lax.rsqrt(variance + 1e-05)
    gain = gain_ref[...]
    bias = bias_ref[...]

    wrow = lax.broadcasted_iota(jnp.int32, (W, C), 0)

    def hidden_row(block, r, keep):
        v = (block.astype(F32) - center) * scale * gain + bias
        h = v / (1.0 + jnp.exp(-v))
        if keep is not None:
            h = jnp.where(keep, h, 0.0)
        rows = pl.ds(r * W, W)
        hcat[rows, 0:C] = jnp.where(wrow == 0, 0.0, pltpu.roll(h, 1, 0)).astype(BF)
        hcat[rows, C : 2 * C] = h.astype(BF)
        hcat[rows, 2 * C : 3 * C] = jnp.where(wrow == W - 1, 0.0, pltpu.roll(h, W - 1, 0)).astype(BF)

    hidden_row(lat[0:W], 1, None)
    hidden_row(lat[W : 2 * W], 2, None)
    loads[2].wait()
    cacc[...] = jnp.dot(hcat[W : W + T], convw[1], preferred_element_type=F32)
    halos[0].wait_recv()
    halos[1].wait_recv()
    hidden_row(halo[0], 0, p > 0)
    hidden_row(halo[1], 3, p < 31)
    cacc[...] += jnp.dot(hcat[0:T], convw[0], preferred_element_type=F32)
    cacc[...] += jnp.dot(hcat[2 * W : 2 * W + T], convw[2], preferred_element_type=F32)
    resid[...] = (lat[...].astype(F32) + cacc[...]).astype(BF)

    loads[3].wait()
    loads[4].wait()
    qbuf[0] = (jnp.dot(resid[...], wqkv[:, 0:HC], preferred_element_type=F32) * SCALE).astype(BF)
    qs_send = [remote(qbuf.at[0], qbuf.at[s], qss.at[s - 1], qrs.at[s - 1], z_peers[s]) for s in (1, 3, 2)]
    for c in qs_send:
        c.start()
    kv[0:T] = jnp.dot(resid[...], wqkv[:, HC:], preferred_element_type=F32).astype(BF)
    fresh_copy = pltpu.make_async_copy(kv.at[pl.ds(0, T)], fresh_h, lsem.at[10])
    fresh_copy.start()

    for i in (0, 1, 2):
        kvs[i].wait_recv()
    fwd = [
        remote(kv.at[pl.ds(1 * T, T)], kv.at[pl.ds(6 * T, T)], kss.at[4], krs.at[4], xy_peers[2]),
        remote(kv.at[pl.ds(3 * T, T)], kv.at[pl.ds(8 * T, T)], kss.at[6], krs.at[6], xy_peers[3]),
        remote(kv.at[pl.ds(2 * T, T)], kv.at[pl.ds(7 * T, T)], kss.at[5], krs.at[5], xy_peers[2]),
    ]
    for c in fwd:
        c.start()
    loads[5].wait()

    lane = lax.broadcasted_iota(jnp.int32, (T, 128), 1)
    first = lane < HEAD
    ones = jnp.ones((CHUNK, 128), BF)

    def scores(qs, row0, h):
        q = qbuf[qs, :, (h // 2) * 128 : (h // 2) * 128 + 128]
        q = jnp.where(first if h % 2 == 0 else ~first, q, jnp.zeros_like(q))
        k = kv[pl.ds(row0, CHUNK), (h // 2) * 128 : (h // 2) * 128 + 128]
        return lax.dot_general(q, k, (((1,), (1,)), ((), ())), preferred_element_type=F32)

    def weigh(row0, h, prob):
        v = kv[pl.ds(row0, CHUNK), HC + (h // 2) * 128 : HC + (h // 2) * 128 + 128]
        return jnp.dot(prob, jnp.concatenate([v, ones], axis=1), preferred_element_type=F32)

    def pipeline(soft, done, qs, row0):
        ss, ps = {}, {}
        for i in range(HEADS + 2):
            if i < HEADS:
                ss[i] = scores(qs, row0, i)
            if 0 <= i - 1 < HEADS:
                ps[i - 1] = soft(ss.pop(i - 1), i - 1)
            if 0 <= i - 2 < HEADS:
                prob, extra = ps.pop(i - 2)
                done(i - 2, weigh(row0, i - 2, prob), extra)

    def first_chunk(t, carry):
        qs = t + (t // 2) * (5 - 2 * t)
        row0 = pl.multiple_of(jnp.where(t == 0, 0, T), T)

        @pl.when(t > 0)
        def _():
            remote(qbuf.at[0], qbuf.at[qs], qss.at[qs - 1], qrs.at[qs - 1], z_peers[1]).wait_recv()

        def soft(s, h):
            top = jnp.max(s, axis=1, keepdims=True)
            mbuf[qs, h] = jnp.broadcast_to(top, (T, 128))
            return jnp.exp2(s - top).astype(BF), None

        held = {}

        def done(h, r, _):
            lbuf[qs, h] = r[:, 128:]
            if h % 2 == 0:
                held[0] = r[:, :128]
            else:
                acc[qs, h // 2] = jnp.where(first, held.pop(0), r[:, :128])

        pipeline(soft, done, qs, row0)
        return carry

    lax.fori_loop(0, 4, first_chunk, 0)

    kvs[3].wait_recv()
    for c in fwd:
        c.wait_recv()

    def second_chunk(t, carry):
        qs = 3 - t
        row0 = 5 * T

        def soft(s, h):
            old = mbuf[qs, h]
            new = jnp.maximum(old, jnp.max(s, axis=1, keepdims=True))
            return jnp.exp2(s - new[:, :1]).astype(BF), (new, jnp.exp2(old - new))

        held = {}
        lses = jnp.zeros((T, 128), F32)

        def done(h, r, extra):
            nonlocal lses
            new, shrink = extra
            tot = lbuf[qs, h] * shrink + r[:, 128:]
            lses = jnp.where(lane == h, new + jnp.log2(tot), lses)
            o = acc[qs, h // 2] * shrink + r[:, :128]
            o = o / tot
            if h % 2 == 0:
                held[0] = o
            else:
                pout[qs, :, (h // 2) * 128 : (h // 2) * 128 + 128] = jnp.where(first, held.pop(0), o).astype(BF)

        pipeline(soft, done, qs, row0)
        lout[qs] = jnp.transpose(lses)[0:8]

        @pl.when(t < 3)
        def _():
            dev = at(x, y, (z + 1 + t) % 4)
            remote(pout.at[qs], pin.at[qs], pss.at[qs], prs.at[qs], dev).start()
            remote(lout.at[qs], lin.at[qs], lss.at[qs], lrs.at[qs], dev).start()

        return carry

    lax.fori_loop(0, 4, second_chunk, 0)

    backs = []
    for s in (3, 2, 1):
        backs.append(remote(pout.at[s], pin.at[s], pss.at[s], prs.at[s], z_back[s]))
        backs.append(remote(lout.at[s], lin.at[s], lss.at[s], lrs.at[s], z_back[s]))
    for c in backs:
        c.wait_recv()

    lse = [lout[0], lin[1], lin[2], lin[3]]
    top = jnp.maximum(jnp.maximum(lse[0], lse[1]), jnp.maximum(lse[2], lse[3]))
    ws = [jnp.exp2(v - top) for v in lse]
    tot = ws[0] + ws[1] + ws[2] + ws[3]
    ws = [jnp.transpose(v / tot) for v in ws]
    pairs = []
    for hp in range(HEADS // 2):
        cols = slice(hp * 128, hp * 128 + 128)
        o = None
        for s in range(4):
            part = (pout[0, :, cols] if s == 0 else pin[s, :, cols]).astype(F32)
            wgt = jnp.where(first, ws[s][:, 2 * hp : 2 * hp + 1], ws[s][:, 2 * hp + 1 : 2 * hp + 2])
            o = part * wgt if o is None else o + part * wgt
        pairs.append(o.astype(BF))
    attn = jnp.concatenate(pairs, axis=1)
    loads[6].wait()
    mixed = (resid[...].astype(F32) + jnp.dot(attn, wout[...], preferred_element_type=F32)).astype(BF)
    resid[...] = mixed
    mixed = mixed.astype(F32)
    mean = jnp.mean(mixed, axis=1, keepdims=True)
    dev = mixed - mean
    var = jnp.mean(dev * dev, axis=1, keepdims=True)
    units[...] = (
        dev * lax.rsqrt(var + 1e-05) * lgain_ref[...] + lbias_ref[...] + code_ref[pl.ds(f, 1), :]
    ).astype(BF)

    def quarter(g):
        return pl.ds(pl.multiple_of(g * QTR, QTR), QTR)

    us = [
        remote(units.at[quarter(f_ids[d])], ubuf.at[pl.ds(d * QTR, QTR)], uss.at[d - 1], urs.at[d - 1], f_peers[d])
        for d in (2, 3, 1)
    ]
    for c in us:
        c.start()
    ubuf[0:QTR] = units[quarter(f)]
    loads[7].wait()
    loads[8].wait()
    for c in us:
        c.wait_recv()
    tqkv = jnp.dot(ubuf[...], wt[...], preferred_element_type=F32).astype(BF).astype(F32)
    ts = []
    for a in range(FRAMES):
        tq = tqkv[a * QTR : (a + 1) * QTR, 0:C]
        his, los = [], []
        for b in range(FRAMES):
            prod = tq * tqkv[b * QTR : (b + 1) * QTR, C : 2 * C]
            phi = prod.astype(BF)
            his.append(phi)
            los.append((prod - phi.astype(F32)).astype(BF))
        lhs = jnp.concatenate([jnp.concatenate(his, axis=0), jnp.concatenate(los, axis=0)], axis=1)
        sc = jnp.dot(lhs, hsum_ref[...], preferred_element_type=F32) * THEAD ** (-0.5)
        sc = [sc[b * QTR : (b + 1) * QTR] for b in range(FRAMES)]
        top = jnp.maximum(jnp.maximum(sc[0], sc[1]), jnp.maximum(sc[2], sc[3]))
        es = [jnp.exp(v - top) for v in sc]
        rec = 1.0 / (es[0] + es[1] + es[2] + es[3])
        rhi = rec.astype(BF)
        rlo = (rec - rhi.astype(F32)).astype(BF)
        wide_rows = jnp.concatenate([e.astype(BF) for e in es] + [rhi, rlo], axis=0)
        ex = jnp.dot(wide_rows, hexp_ref[...], preferred_element_type=F32)
        o = None
        for b in range(FRAMES):
            term = ex[b * QTR : (b + 1) * QTR] * tqkv[b * QTR : (b + 1) * QTR, 2 * C : 3 * C]
            o = term if o is None else o + term
        o = o * (ex[4 * QTR : 5 * QTR] + ex[5 * QTR : 6 * QTR])
        if a == 0:
            tbuf[quarter(f), :] = o.astype(BF)
        else:
            tres[a] = o.astype(BF)
            ts.append(remote(tres.at[a], tbuf.at[quarter(f)], tss.at[a - 1], trs.at[a - 1], f_peers[a]))
            ts[-1].start()
    tback = [remote(tres.at[d], tbuf.at[quarter(f_ids[d])], tss.at[d - 1], trs.at[d - 1], f_peers[d]) for d in (1, 2, 3)]
    loads[9].wait()
    for c in tback:
        c.wait_recv()
    out_ref[...] = resid[...].astype(F32) + jnp.dot(tbuf[...], tout[...], preferred_element_type=F32)

    fresh_copy.wait()
    for c in st1 + halos + kvs + st2 + qs_send + fwd + backs + us + ts:
        c.wait_send()


def codes():
    halves = np.arange(C // 2, dtype=np.float64)
    freqs = np.exp(-math.log(10000.0) * 2.0 * halves / C)
    angles = np.arange(FRAMES)[:, None] * freqs[None, :]
    table = np.stack([np.sin(angles), np.cos(angles)], axis=-1).reshape(FRAMES, C)
    return np.concatenate([table, np.zeros((8 - FRAMES, C))]).astype(np.float32)


def shards(
    latent, gn_gain, gn_bias, conv_weight, w_query, w_kv, w_out, stale_kv, ln_gain, ln_bias, t_query, t_kv, t_out
):
    group = np.arange(C) // (C // GROUPS)
    gmat = jnp.asarray((group[:, None] == group[None, :]).astype(np.float32), BF)
    head = (np.arange(C)[:, None] // THEAD == np.arange(128)[None, :]).astype(np.float32)
    hsum = jnp.asarray(np.concatenate([head, head]), BF)
    hexp = jnp.asarray(head.T.copy(), BF)
    hbm = pl.BlockSpec(memory_space=pl.ANY)
    vmem = pl.BlockSpec(memory_space=pltpu.VMEM)
    dma = pltpu.SemaphoreType.DMA
    out, fresh = pl.pallas_call(
        kernel,
        out_shape=(jax.ShapeDtypeStruct((T, C), F32), jax.ShapeDtypeStruct((T, 2 * HC), BF)),
        in_specs=[hbm] * 9 + [vmem] * 5 + [hbm] + [vmem] * 2,
        out_specs=(vmem, hbm),
        scratch_shapes=[
            pltpu.VMEM((T, C), BF),
            pltpu.VMEM((2, W, C), BF),
            pltpu.VMEM((3, 3 * C, C), BF),
            pltpu.VMEM((C, 3 * HC), BF),
            pltpu.VMEM((HC, C), BF),
            pltpu.VMEM((C, 3 * C), BF),
            pltpu.VMEM((C, C), BF),
            pltpu.VMEM((C, C), BF),
            pltpu.VMEM((4 * W, 3 * C), BF),
            pltpu.VMEM((T, C), F32),
            pltpu.VMEM((T, C), BF),
            pltpu.VMEM((8, 2, C), F32),
            pltpu.VMEM((4, 2, C), F32),
            pltpu.VMEM((4, T, HC), BF),
            pltpu.VMEM((9 * T, 2 * HC), BF),
            pltpu.VMEM((4, HEADS // 2, T, 128), F32),
            pltpu.VMEM((4, HEADS, T, 128), F32),
            pltpu.VMEM((4, HEADS, T, 128), F32),
            pltpu.VMEM((4, T, HC), BF),
            pltpu.VMEM((4, T, HC), BF),
            pltpu.VMEM((4, 8, T), F32),
            pltpu.VMEM((4, 8, T), F32),
            pltpu.VMEM((T, C), BF),
            pltpu.VMEM((T, C), BF),
            pltpu.VMEM((4, QTR, C), BF),
            pltpu.VMEM((T, C), BF),
            dma((11,)), dma((2,)), dma((2,)), dma((7,)), dma((7,)), dma((3,)), dma((3,)),
            dma((7,)), dma((7,)), dma((3,)), dma((3,)), dma((4,)), dma((4,)), dma((4,)), dma((4,)),
            dma((3,)), dma((3,)), dma((3,)), dma((3,)),
        ],
        compiler_params=pltpu.CompilerParams(
            collective_id=0, has_side_effects=True, vmem_limit_bytes=63 * 2**20
        ),
    )(
        latent.reshape(T, C),
        stale_kv.reshape(T, 2 * HC),
        conv_weight.reshape(3, 3 * C, C),
        w_query,
        w_kv,
        w_out,
        t_query,
        t_kv,
        t_out,
        gn_gain.reshape(1, C),
        gn_bias.reshape(1, C),
        ln_gain.reshape(1, C),
        ln_bias.reshape(1, C),
        jnp.asarray(codes()),
        gmat,
        hsum,
        hexp,
    )
    return out.reshape(1, 2, W, C), fresh.reshape(1, 2, W, 2 * HC)


def solution(mesh):
    sharded = P("frame", "patch", None, None)
    placed = (sharded,) + (P(),) * 6 + (sharded,) + (P(),) * 5
    return jax.shard_map(
        shards, mesh=mesh, in_specs=placed, out_specs=(sharded, sharded), check_vma=False
    )
```

time: 481 us -> 133 us (0.28)
  the two profiles are of different devices: /device:TPU:1 before, /device:TPU:122 now
where the time goes in v1:
time: 133 us
  Pallas kernels  123 us (92%)
  local copies, waits for them, and re-layouts  9.19 us (7%)
    pallas_call x1, Pallas kernels, shards(): pl.pallas_call(kernel, out_shape=(jax.ShapeDtypeStruct((T, C), F32), jax....  123 us
    unnamed x2, local copies, waits for them, and re-layouts  4.13 us

profile of v1, /device:TPU:122, one launch (start us, length us, event | category | flops | bytes accessed | tf_op | source)
XLA Modules:
  0.0 132.9 jit_solution(8428009875163355404)
XLA Ops:
  0.6 1.3 reshape.34.gain_ref
  1.9 1.3 reshape.35.bias_ref
  3.2 1.3 reshape.36.lgain_ref
  4.4 1.3 reshape.37.lbias_ref
  5.7 123.0 %shard_map.176 = (f32[384,640]{1,0:T(8,128)}, bf16[384,768]{1,0:T(8,128)(2,1)}) custom-call(bf16[384,640]{1,0:T(8,128)(2,1)} %bitcast.9, bf16[384,768]{1,0:T(8,128)(2,1)} %bitcast.7, bf16[3,1920,640]{2,1,0:T(8,128)(2,1)} %bitcast.5, bf16[640,384]{1,0:T(8,128)(2,1)} %wq_h.1, bf16[640,768]{1,0:T(8,128)(2,1)} %wkv_h.1, bf16[384,640]{1,0:T(8,128)(2,1)} %wout_h.1, ...), custom_call_target="tpu_custom_call" | custom-call | tf_op jit(solution)/shard_map/pallas_call | solution.py:376
  128.7 2.2 %copy.21 = f32[1,2,192,640]{3,2,1,0:T(8,128)} copy(f32[1,2,192,640]{3,2,1,0:T(8,128)} %bitcast.6) | data formatting | bytes 1966080
  130.9 1.9 %copy.22 = bf16[1,2,192,768]{3,2,1,0:T(8,128)(2,1)} copy(bf16[1,2,192,768]{3,2,1,0:T(8,128)(2,1)} %bitcast.8) | data formatting | bytes 1179648

commit v2 on v1

v2 whole, which is shorter than its diff:
```python
import math

import jax
import jax.numpy as jnp
import numpy as np
from jax import lax
from jax.experimental import pallas as pl
from jax.experimental.pallas import tpu as pltpu
from jax.sharding import PartitionSpec as P

C = 640
THEADS = 8
GROUPS = 32
HEADS = 6
HEAD = 64
THEAD = 80
HC = 384
W = 192
T = 384
FRAMES = 4
HALF = 192
QTR = 48
LSE = 256
CHUNK = 1536
BF = jnp.bfloat16
F32 = jnp.float32
SCALE = HEAD ** (-0.5) * math.log2(math.e)
MESH = pl.DeviceIdType.MESH


def kernel(
    lat_h, stale_h, convw_h, wq_h, wkv_h, wout_h, tq_h, tkv_h, tout_h,
    gain_ref, bias_ref, lgain_ref, lbias_ref, code_ref, gmat_h, hsum_ref, hexp_ref,
    out_ref, fresh_h,
    lat, halo, convw, wqkv, wout, wt, tout, gmat, hcat, cacc, resid,
    stat1, stat2, qbuf, kv, acc, lbuf, mbuf, pout, pin, lout, lin,
    units, ubuf, tres, tbuf,
    lsem, hss, hrs, s1s, s1r, s2s, s2r, kss, krs, qss, qrs, pss, prs, lss, lrs, uss, urs, tss, trs,
):
    f = lax.axis_index("frame")
    p = lax.axis_index("patch")
    x = p // 16
    y = (p // 4) % 4
    z = p % 4

    def at(px, py, pz):
        return (f, px * 16 + py * 4 + pz)

    def remote(src, dst, ss, rs, dev):
        return pltpu.make_async_remote_copy(
            src_ref=src, dst_ref=dst, send_sem=ss, recv_sem=rs, device_id=dev, device_id_type=MESH
        )

    xy = [((x + dx) % 2, (y + dy) % 4) for dx, dy in ((0, 1), (0, 3), (1, 0), (0, 2), (1, 1), (1, 3), (1, 2))]
    xy_peers = [at(a, b, z) for a, b in xy]
    y_up, y_down, x_other = xy_peers[:3]
    z_peers = {s: at(x, y, (z + s) % 4) for s in (1, 2, 3)}
    z_back = {s: at(x, y, (z + 4 - s) % 4) for s in (1, 2, 3)}
    up = (f, (p + 1) % 32)
    down = (f, (p + 31) % 32)
    f_ids = {0: f, 1: f + 1 - 2 * (f % 2), 2: (f + 2) % 4, 3: 3 - f}
    f_peers = {d: (f_ids[d], p) for d in (1, 2, 3)}

    loads = [
        pltpu.make_async_copy(lat_h, lat, lsem.at[0]),
        pltpu.make_async_copy(gmat_h, gmat, lsem.at[1]),
        pltpu.make_async_copy(convw_h, convw, lsem.at[2]),
        pltpu.make_async_copy(wq_h, wqkv.at[:, pl.ds(0, HC)], lsem.at[3]),
        pltpu.make_async_copy(wkv_h, wqkv.at[:, pl.ds(HC, 2 * HC)], lsem.at[4]),
        pltpu.make_async_copy(stale_h, kv.at[pl.ds(4 * T, T)], lsem.at[5]),
        pltpu.make_async_copy(wout_h, wout, lsem.at[6]),
        pltpu.make_async_copy(tq_h, wt.at[:, pl.ds(0, C)], lsem.at[7]),
        pltpu.make_async_copy(tkv_h, wt.at[:, pl.ds(C, 2 * C)], lsem.at[8]),
        pltpu.make_async_copy(tout_h, tout, lsem.at[9]),
    ]
    for c in loads:
        c.start()

    barrier = pltpu.get_barrier_semaphore()
    greet = xy_peers + list(z_peers.values()) + [up, down] + list(f_peers.values())
    for dev in greet:
        pl.semaphore_signal(barrier, inc=1, device_id=dev, device_id_type=MESH)

    row8 = lax.broadcasted_iota(jnp.int32, (8, C), 0)
    loads[0].wait()
    wide = lat[...].astype(F32)
    stat1[0, 0:1, :] = jnp.sum(wide, axis=0, keepdims=True)
    stat1[0, 1:2, :] = jnp.sum(wide * wide, axis=0, keepdims=True)
    pl.semaphore_wait(barrier, len(greet))

    st1 = [remote(stat1.at[0], stat1.at[1 + i], s1s.at[i], s1r.at[i], d) for i, d in enumerate(xy_peers)]
    for c in st1:
        c.start()
    halos = [
        remote(lat_h.at[pl.ds(W, W)], halo.at[0], hss.at[0], hrs.at[0], up),
        remote(lat_h.at[pl.ds(0, W)], halo.at[1], hss.at[1], hrs.at[1], down),
    ]
    for c in halos:
        c.start()

    def block(s, low=0, rows=T):
        return kv.at[pl.ds(s * T + low, rows)]

    def passed(i, src, dst, low, rows, dev):
        return remote(block(src, low, rows), block(dst, low, rows), kss.at[i], krs.at[i], dev)

    wave1 = [
        remote(stale_h, block(1), kss.at[0], krs.at[0], y_up),
        remote(stale_h, block(2), kss.at[1], krs.at[1], y_down),
        remote(stale_h, block(3), kss.at[2], krs.at[2], x_other),
    ]
    wave2 = [
        passed(3, 1, 6, 128, 64, x_other),
        passed(5, 3, 6, 0, 128, y_up),
        passed(6, 3, 7, 256, 128, y_down),
        passed(4, 2, 7, 192, 64, x_other),
        passed(7, 1, 5, 0, 192, y_up),
        passed(8, 2, 5, 192, 192, y_down),
        passed(9, 1, 6, 192, 192, x_other),
        passed(10, 2, 7, 0, 192, x_other),
    ]
    wave3 = [
        passed(11, 6, 8, 0, 192, y_up),
        passed(12, 7, 8, 192, 192, y_down),
    ]
    for c in wave1:
        c.start()

    for c in st1:
        c.wait_recv()
    stat2[0] = jnp.sum(stat1[...], axis=0)
    st2 = [remote(stat2.at[0], stat2.at[s], s2s.at[s - 1], s2r.at[s - 1], z_peers[s]) for s in (1, 3, 2)]
    for c in st2:
        c.start()
    loads[1].wait()
    for c in st2:
        c.wait_recv()
    total = jnp.sum(stat2[...], axis=0)
    total8 = jnp.where(row8 == 0, total[0:1], jnp.where(row8 == 1, total[1:2], 0.0))
    hi = total8.astype(BF).astype(F32)
    mid = (total8 - hi).astype(BF).astype(F32)
    low = total8 - hi - mid
    parts = jnp.concatenate([hi, mid, low, jnp.zeros((8, C), F32)], axis=0).astype(BF)
    summed = jnp.dot(parts, gmat[...], preferred_element_type=F32)
    summed = summed[0:8] + summed[8:16] + summed[16:24]
    count = float(32 * T * (C // GROUPS))
    center = summed[0:1] / count
    variance = summed[1:2] / count - center * center
    scale = lax.rsqrt(variance + 1e-05)
    gain = gain_ref[...].reshape(1, C)
    bias = bias_ref[...].reshape(1, C)

    wrow = lax.broadcasted_iota(jnp.int32, (W, C), 0)

    def hidden_row(block, r, keep):
        v = (block.astype(F32) - center) * scale * gain + bias
        h = v / (1.0 + jnp.exp(-v))
        if keep is not None:
            h = jnp.where(keep, h, 0.0)
        rows = pl.ds(r * W, W)
        hcat[rows, 0:C] = jnp.where(wrow == 0, 0.0, pltpu.roll(h, 1, 0)).astype(BF)
        hcat[rows, C : 2 * C] = h.astype(BF)
        hcat[rows, 2 * C : 3 * C] = jnp.where(wrow == W - 1, 0.0, pltpu.roll(h, W - 1, 0)).astype(BF)

    hidden_row(lat[0:W], 1, None)
    hidden_row(lat[W : 2 * W], 2, None)
    loads[2].wait()
    cacc[...] = jnp.dot(hcat[W : W + T], convw[1], preferred_element_type=F32)
    halos[0].wait_recv()
    halos[1].wait_recv()
    hidden_row(halo[0], 0, p > 0)
    hidden_row(halo[1], 3, p < 31)
    cacc[...] += jnp.dot(hcat[0:T], convw[0], preferred_element_type=F32)
    cacc[...] += jnp.dot(hcat[2 * W : 2 * W + T], convw[2], preferred_element_type=F32)
    resid[...] = (lat[...].astype(F32) + cacc[...]).astype(BF)

    def half(h):
        return pl.ds(pl.multiple_of(h * HALF, HALF), HALF)

    def q_copy(s, h, dev, src=0):
        i = (s - 1) * 2 + h
        return remote(qbuf.at[src, half(h)], qbuf.at[s, half(h)], qss.at[i], qrs.at[i], dev)

    loads[3].wait()
    loads[4].wait()
    qbuf[0] = (jnp.dot(resid[...], wqkv[:, 0:HC], preferred_element_type=F32) * SCALE).astype(BF)
    q_sends = [q_copy(s, h, z_peers[s]) for h in (0, 1) for s in (1, 3)]
    for c in q_sends:
        c.start()
    kv[0:T] = jnp.dot(resid[...], wqkv[:, HC:], preferred_element_type=F32).astype(BF)
    fresh_copy = pltpu.make_async_copy(kv.at[pl.ds(0, T)], fresh_h, lsem.at[10])
    fresh_copy.start()

    for c in wave1:
        c.wait_recv()
    for c in wave2:
        c.start()
    loads[5].wait()

    lane = lax.broadcasted_iota(jnp.int32, (HALF, 128), 1)
    first = lane < HEAD
    ones = jnp.ones((CHUNK, 128), BF)

    def scores(qs, rows, row0, h):
        q = qbuf[qs, rows, (h // 2) * 128 : (h // 2) * 128 + 128]
        q = jnp.where(first if h % 2 == 0 else ~first, q, jnp.zeros_like(q))
        k = kv[pl.ds(row0, CHUNK), (h // 2) * 128 : (h // 2) * 128 + 128]
        return lax.dot_general(q, k, (((1,), (1,)), ((), ())), preferred_element_type=F32)

    def weigh(row0, h, prob):
        v = kv[pl.ds(row0, CHUNK), HC + (h // 2) * 128 : HC + (h // 2) * 128 + 128]
        return jnp.dot(prob, jnp.concatenate([v, ones], axis=1), preferred_element_type=F32)

    def pipeline(soft, done, qs, rows, row0):
        ss, ps = {}, {}
        for i in range(HEADS + 2):
            if i < HEADS:
                ss[i] = scores(qs, rows, row0, i)
            if 0 <= i - 1 < HEADS:
                ps[i - 1] = soft(ss.pop(i - 1), i - 1)
            if 0 <= i - 2 < HEADS:
                prob, extra = ps.pop(i - 2)
                done(i - 2, weigh(row0, i - 2, prob), extra)

    def first_chunk(t, carry):
        qs = jnp.where(t < 2, 0, jnp.where(t < 6, 1 + 2 * (t % 2), 2))
        hh = jnp.where(t < 2, t, jnp.where(t < 6, (t - 2) // 2, t - 6))
        rows = half(hh)
        row0 = pl.multiple_of(jnp.where(t < 2, 0, T), T)

        @pl.when(t >= 2)
        def _():
            q_copy(qs, hh, z_peers[1]).wait_recv()

        @pl.when((t == 2) | (t == 4))
        def _():
            q_copy(2, hh, z_peers[1], src=1).start()

        @pl.when(t == 4)
        def _():
            for c in wave2[:4]:
                c.wait_recv()
            for c in wave3:
                c.start()

        def soft(s, h):
            top = jnp.max(s, axis=1, keepdims=True)
            mbuf[qs, h, rows] = jnp.broadcast_to(top, (HALF, 128))
            return jnp.exp2(s - top).astype(BF), None

        held = {}

        def done(h, r, _):
            lbuf[qs, h, rows] = r[:, 128:]
            if h % 2 == 0:
                held[0] = r[:, :128]
            else:
                acc[qs, h // 2, rows] = jnp.where(first, held.pop(0), r[:, :128])

        pipeline(soft, done, qs, rows, row0)
        return carry

    lax.fori_loop(0, 8, first_chunk, 0)

    for c in wave2[4:] + wave3:
        c.wait_recv()

    def part_copies(s, h, dev):
        i = s * 2 + h
        return [
            remote(pout.at[s, half(h)], pin.at[s, half(h)], pss.at[i], prs.at[i], dev),
            remote(lout.at[s, h], lin.at[s, h], lss.at[i], lrs.at[i], dev),
        ]

    def quarter(h, g):
        return pl.ds(pl.multiple_of(h * HALF + g * QTR, QTR), QTR)

    def unit_copy(d, h):
        i = (d - 1) * 2 + h
        return remote(units.at[quarter(h, f_ids[d])], ubuf.at[quarter(h, d)], uss.at[i], urs.at[i], f_peers[d])

    def back_copy(d, h, owner):
        i = (d - 1) * 2 + h
        return remote(tres.at[h, d], tbuf.at[quarter(h, owner)], tss.at[i], trs.at[i], f_peers[d])

    def combine(h):
        rows = half(h)
        for s in (3, 2, 1):
            for c in part_copies(s, h, z_back[s]):
                c.wait_recv()
        lse = [lout[0, h], lin[1, h], lin[2, h], lin[3, h]]
        top = jnp.maximum(jnp.maximum(lse[0], lse[1]), jnp.maximum(lse[2], lse[3]))
        ws = [jnp.exp2(v - top) for v in lse]
        tot = ws[0] + ws[1] + ws[2] + ws[3]
        ws = [jnp.transpose(v / tot)[0:HALF] for v in ws]
        pairs = []
        for hp in range(HEADS // 2):
            cols = slice(hp * 128, hp * 128 + 128)
            o = None
            for s in range(4):
                part = (pout[0, rows, cols] if s == 0 else pin[s, rows, cols]).astype(F32)
                wgt = jnp.where(first, ws[s][:, 2 * hp : 2 * hp + 1], ws[s][:, 2 * hp + 1 : 2 * hp + 2])
                o = part * wgt if o is None else o + part * wgt
            pairs.append(o.astype(BF))
        attn = jnp.concatenate(pairs, axis=1)
        mixed = (resid[rows].astype(F32) + jnp.dot(attn, wout[...], preferred_element_type=F32)).astype(BF)
        resid[rows] = mixed
        mixed = mixed.astype(F32)
        mean = jnp.mean(mixed, axis=1, keepdims=True)
        dev = mixed - mean
        var = jnp.mean(dev * dev, axis=1, keepdims=True)
        lgain = lgain_ref[...].reshape(1, C)
        lbias = lbias_ref[...].reshape(1, C)
        units[rows] = (dev * lax.rsqrt(var + 1e-05) * lgain + lbias + code_ref[pl.ds(f, 1), :]).astype(BF)
        for d in (2, 3, 1):
            unit_copy(d, h).start()
        ubuf[quarter(h, 0)] = units[quarter(h, f)]

    def temporal(h):
        for d in (1, 2, 3):
            unit_copy(d, h).wait_recv()
        tqkv = jnp.dot(ubuf[half(h)], wt[...], preferred_element_type=F32).astype(BF).astype(F32)
        for a in (2, 3, 1, 0):
            tq = tqkv[a * QTR : (a + 1) * QTR, 0:C]
            his, los = [], []
            for b in range(FRAMES):
                prod = tq * tqkv[b * QTR : (b + 1) * QTR, C : 2 * C]
                phi = prod.astype(BF)
                his.append(phi)
                los.append((prod - phi.astype(F32)).astype(BF))
            lhs = jnp.concatenate([jnp.concatenate(his, axis=0), jnp.concatenate(los, axis=0)], axis=1)
            sc = jnp.dot(lhs, hsum_ref[...], preferred_element_type=F32) * THEAD ** (-0.5)
            sc = [sc[b * QTR : (b + 1) * QTR] for b in range(FRAMES)]
            top = jnp.maximum(jnp.maximum(sc[0], sc[1]), jnp.maximum(sc[2], sc[3]))
            es = [jnp.exp(v - top) for v in sc]
            rec = 1.0 / (es[0] + es[1] + es[2] + es[3])
            rhi = rec.astype(BF)
            rlo = (rec - rhi.astype(F32)).astype(BF)
            wide_rows = jnp.concatenate([e.astype(BF) for e in es] + [rhi, rlo], axis=0)
            ex = jnp.dot(wide_rows, hexp_ref[...], preferred_element_type=F32)
            o = None
            for b in range(FRAMES):
                term = ex[b * QTR : (b + 1) * QTR] * tqkv[b * QTR : (b + 1) * QTR, 2 * C : 3 * C]
                o = term if o is None else o + term
            o = (o * (ex[4 * QTR : 5 * QTR] + ex[5 * QTR : 6 * QTR])).astype(BF)
            if a == 0:
                tbuf[quarter(h, f)] = o
            else:
                tres[h, a] = o
                back_copy(a, h, f).start()

    def finish(h):
        for d in (1, 2, 3):
            back_copy(d, h, f_ids[d]).wait_recv()
        rows = half(h)
        out_ref[rows] = resid[rows].astype(F32) + jnp.dot(tbuf[rows], tout[...], preferred_element_type=F32)

    for i in (6, 7, 8, 9):
        loads[i].wait()

    def second_chunk(t, carry):
        hh = t // 4
        qs = 3 - t % 4
        rows = half(hh)
        row0 = 5 * T

        def soft(s, h):
            old = mbuf[qs, h, rows]
            new = jnp.maximum(old, jnp.max(s, axis=1, keepdims=True))
            return jnp.exp2(s - new[:, :1]).astype(BF), (new, jnp.exp2(old - new))

        held = {}
        lses = jnp.zeros((HALF, 128), F32)

        def done(h, r, extra):
            nonlocal lses
            new, shrink = extra
            tot = lbuf[qs, h, rows] * shrink + r[:, 128:]
            lses = jnp.where(lane == h, new + jnp.log2(tot), lses)
            o = acc[qs, h // 2, rows] * shrink + r[:, :128]
            o = o / tot
            if h % 2 == 0:
                held[0] = o
            else:
                pout[qs, rows, (h // 2) * 128 : (h // 2) * 128 + 128] = jnp.where(first, held.pop(0), o).astype(BF)

        pipeline(soft, done, qs, rows, row0)
        lses = jnp.concatenate([lses, jnp.zeros((LSE - HALF, 128), F32)], axis=0)
        lout[qs, hh] = jnp.transpose(lses)[0:8]

        @pl.when(qs > 0)
        def _():
            for c in part_copies(qs, hh, at(x, y, (z + 4 - qs) % 4)):
                c.start()

        @pl.when(t == 4)
        def _():
            combine(0)

        @pl.when(t == 6)
        def _():
            temporal(0)

        return carry

    lax.fori_loop(0, 8, second_chunk, 0)
    combine(1)
    temporal(1)
    finish(0)
    finish(1)

    fresh_copy.wait()
    for c in st1 + halos + wave1 + wave2 + wave3 + st2 + q_sends:
        c.wait_send()
    for h in (0, 1):
        q_copy(2, h, z_peers[1], src=1).wait_send()
        for s in (1, 2, 3):
            for c in part_copies(s, h, z_back[s]):
                c.wait_send()
            unit_copy(s, h).wait_send()
            back_copy(s, h, f).wait_send()


def codes():
    halves = np.arange(C // 2, dtype=np.float64)
    freqs = np.exp(-math.log(10000.0) * 2.0 * halves / C)
    angles = np.arange(FRAMES)[:, None] * freqs[None, :]
    table = np.stack([np.sin(angles), np.cos(angles)], axis=-1).reshape(FRAMES, C)
    return np.concatenate([table, np.zeros((8 - FRAMES, C))]).astype(np.float32)


def shards(
    latent, gn_gain, gn_bias, conv_weight, w_query, w_kv, w_out, stale_kv, ln_gain, ln_bias, t_query, t_kv, t_out
):
    group = np.arange(C) // (C // GROUPS)
    gmat = jnp.asarray((group[:, None] == group[None, :]).astype(np.float32), BF)
    head = (np.arange(C)[:, None] // THEAD == np.arange(128)[None, :]).astype(np.float32)
    hsum = jnp.asarray(np.concatenate([head, head]), BF)
    hexp = jnp.asarray(head.T.copy(), BF)
    hbm = pl.BlockSpec(memory_space=pl.ANY)
    vmem = pl.BlockSpec(memory_space=pltpu.VMEM)
    dma = pltpu.SemaphoreType.DMA
    out, fresh = pl.pallas_call(
        kernel,
        out_shape=(jax.ShapeDtypeStruct((T, C), F32), jax.ShapeDtypeStruct((T, 2 * HC), BF)),
        in_specs=[hbm] * 9 + [vmem] * 5 + [hbm] + [vmem] * 2,
        out_specs=(vmem, hbm),
        scratch_shapes=[
            pltpu.VMEM((T, C), BF),
            pltpu.VMEM((2, W, C), BF),
            pltpu.VMEM((3, 3 * C, C), BF),
            pltpu.VMEM((C, 3 * HC), BF),
            pltpu.VMEM((HC, C), BF),
            pltpu.VMEM((C, 3 * C), BF),
            pltpu.VMEM((C, C), BF),
            pltpu.VMEM((C, C), BF),
            pltpu.VMEM((4 * W, 3 * C), BF),
            pltpu.VMEM((T, C), F32),
            pltpu.VMEM((T, C), BF),
            pltpu.VMEM((8, 2, C), F32),
            pltpu.VMEM((4, 2, C), F32),
            pltpu.VMEM((4, T, HC), BF),
            pltpu.VMEM((9 * T, 2 * HC), BF),
            pltpu.VMEM((4, HEADS // 2, T, 128), F32),
            pltpu.VMEM((4, HEADS, T, 128), F32),
            pltpu.VMEM((4, HEADS, T, 128), F32),
            pltpu.VMEM((4, T, HC), BF),
            pltpu.VMEM((4, T, HC), BF),
            pltpu.VMEM((4, 2, 8, LSE), F32),
            pltpu.VMEM((4, 2, 8, LSE), F32),
            pltpu.VMEM((T, C), BF),
            pltpu.VMEM((T, C), BF),
            pltpu.VMEM((2, 4, QTR, C), BF),
            pltpu.VMEM((T, C), BF),
            dma((11,)), dma((2,)), dma((2,)), dma((7,)), dma((7,)), dma((3,)), dma((3,)),
            dma((13,)), dma((13,)), dma((6,)), dma((6,)), dma((8,)), dma((8,)), dma((8,)), dma((8,)),
            dma((6,)), dma((6,)), dma((6,)), dma((6,)),
        ],
        compiler_params=pltpu.CompilerParams(
            collective_id=0, has_side_effects=True, vmem_limit_bytes=63 * 2**20
        ),
    )(
        latent.reshape(T, C),
        stale_kv.reshape(T, 2 * HC),
        conv_weight.reshape(3, 3 * C, C),
        w_query,
        w_kv,
        w_out,
        t_query,
        t_kv,
        t_out,
        gn_gain,
        gn_bias,
        ln_gain,
        ln_bias,
        jnp.asarray(codes()),
        gmat,
        hsum,
        hexp,
    )
    return out.reshape(1, 2, W, C), fresh.reshape(1, 2, W, 2 * HC)


def solution(mesh):
    sharded = P("frame", "patch", None, None)
    placed = (sharded,) + (P(),) * 6 + (sharded,) + (P(),) * 5
    return jax.shard_map(
        shards, mesh=mesh, in_specs=placed, out_specs=(sharded, sharded), check_vma=False
    )
```

time: 133 us -> 94.9 us (0.71)
  the two profiles are of different devices: /device:TPU:122 before, /device:TPU:1 now
where the time goes in v2:
time: 94.9 us; the launch traced here: 94.6 us
  Pallas kernels  89.9 us (95%)
  local copies, waits for them, and re-layouts  4.13 us (4%)
    pallas_call x1, Pallas kernels, shards(): pl.pallas_call(kernel, out_shape=(jax.ShapeDtypeStruct((T, C), F32), jax....  89.9 us
    unnamed x2, local copies, waits for them, and re-layouts  4.13 us

profile of v2, /device:TPU:1, one launch (start us, length us, event | category | flops | bytes accessed | tf_op | source)
XLA Modules:
  0.0 94.6 jit_solution(15406010504717265649)
XLA Ops:
  0.6 89.9 %shard_map.176 = (f32[384,640]{1,0:T(8,128)}, bf16[384,768]{1,0:T(8,128)(2,1)}) custom-call(bf16[384,640]{1,0:T(8,128)(2,1)} %bitcast.9, bf16[384,768]{1,0:T(8,128)(2,1)} %bitcast.7, bf16[3,1920,640]{2,1,0:T(8,128)(2,1)} %bitcast.5, bf16[640,384]{1,0:T(8,128)(2,1)} %wq_h.1, bf16[640,768]{1,0:T(8,128)(2,1)} %wkv_h.1, bf16[384,640]{1,0:T(8,128)(2,1)} %wout_h.1, ...), custom_call_target="tpu_custom_call" | custom-call | tf_op jit(solution)/shard_map/pallas_call | solution.py:443
  90.5 2.2 %copy.21 = f32[1,2,192,640]{3,2,1,0:T(8,128)} copy(f32[1,2,192,640]{3,2,1,0:T(8,128)} %bitcast.6) | data formatting | bytes 1966080
  92.7 1.9 %copy.22 = bf16[1,2,192,768]{3,2,1,0:T(8,128)(2,1)} copy(bf16[1,2,192,768]{3,2,1,0:T(8,128)(2,1)} %bitcast.8) | data formatting | bytes 1179648

commit v3 on v2

--- a/solution.py
+++ b/solution.py
@@ -21,6 +21,7 @@
 HALF = 192
 QTR = 48
 LSE = 256
+PARTS = 4
 CHUNK = 1536
 BF = jnp.bfloat16
 F32 = jnp.float32
@@ -30,11 +31,11 @@
 
 def kernel(
     lat_h, stale_h, convw_h, wq_h, wkv_h, wout_h, tq_h, tkv_h, tout_h,
-    gain_ref, bias_ref, lgain_ref, lbias_ref, code_ref, gmat_h, hsum_ref, hexp_ref,
+    gain_ref, bias_ref, lgain_ref, lbias_ref, code_ref, gmat_h, hsum_h, hexp_h,
     out_ref, fresh_h,
     lat, halo, convw, wqkv, wout, wt, tout, gmat, hcat, cacc, resid,
     stat1, stat2, qbuf, kv, acc, lbuf, mbuf, pout, pin, lout, lin,
-    units, ubuf, tres, tbuf,
+    units, ubuf, tres, tbuf, hsum_ref, hexp_ref,
     lsem, hss, hrs, s1s, s1r, s2s, s2r, kss, krs, qss, qrs, pss, prs, lss, lrs, uss, urs, tss, trs,
 ):
     f = lax.axis_index("frame")
@@ -72,6 +73,8 @@
         pltpu.make_async_copy(tq_h, wt.at[:, pl.ds(0, C)], lsem.at[7]),
         pltpu.make_async_copy(tkv_h, wt.at[:, pl.ds(C, 2 * C)], lsem.at[8]),
         pltpu.make_async_copy(tout_h, tout, lsem.at[9]),
+        pltpu.make_async_copy(hsum_h, hsum_ref, lsem.at[11]),
+        pltpu.make_async_copy(hexp_h, hexp_ref, lsem.at[12]),
     ]
     for c in loads:
         c.start()
@@ -355,12 +358,12 @@
         rows = half(h)
         out_ref[rows] = resid[rows].astype(F32) + jnp.dot(tbuf[rows], tout[...], preferred_element_type=F32)
 
-    for i in (6, 7, 8, 9):
+    for i in (6, 7, 8, 9, 10, 11):
         loads[i].wait()
 
     def second_chunk(t, carry):
-        hh = t // 4
-        qs = 3 - t % 4
+        qs = jnp.where(t < 6, 3 - t % 3, 0)
+        hh = jnp.where(t < 6, t // 3, t - 6)
         rows = half(hh)
         row0 = 5 * T
 
@@ -393,18 +396,15 @@
             for c in part_copies(qs, hh, at(x, y, (z + 4 - qs) % 4)):
                 c.start()
 
-        @pl.when(t == 4)
+        @pl.when(t == 6)
         def _():
             combine(0)
 
-        @pl.when(t == 6)
-        def _():
-            temporal(0)
-
         return carry
 
     lax.fori_loop(0, 8, second_chunk, 0)
     combine(1)
+    temporal(0)
     temporal(1)
     finish(0)
     finish(1)
@@ -419,6 +419,26 @@
                 c.wait_send()
             unit_copy(s, h).wait_send()
             back_copy(s, h, f).wait_send()
+
+
+def deliver(out_in, fresh_in, out, fresh, held_out, held_fresh, sems):
+    steps = []
+    for i in range(PARTS):
+        rows = pl.ds(i * (T // PARTS), T // PARTS)
+        for k, (src, held, dst) in enumerate(((out_in, held_out, out), (fresh_in, held_fresh, fresh))):
+            steps.append(
+                (
+                    pltpu.make_async_copy(src.at[rows], held.at[rows], sems.at[k, i]),
+                    pltpu.make_async_copy(held.at[rows], dst.at[rows], sems.at[2 + k, i]),
+                )
+            )
+    for load, _ in steps:
+        load.start()
+    for load, store in steps:
+        load.wait()
+        store.start()
+    for _, store in steps:
+        store.wait()
 
 
 def codes():
@@ -443,7 +463,7 @@
     out, fresh = pl.pallas_call(
         kernel,
         out_shape=(jax.ShapeDtypeStruct((T, C), F32), jax.ShapeDtypeStruct((T, 2 * HC), BF)),
-        in_specs=[hbm] * 9 + [vmem] * 5 + [hbm] + [vmem] * 2,
+        in_specs=[hbm] * 9 + [vmem] * 5 + [hbm] * 3,
         out_specs=(vmem, hbm),
         scratch_shapes=[
             pltpu.VMEM((T, C), BF),
@@ -472,7 +492,9 @@
             pltpu.VMEM((T, C), BF),
             pltpu.VMEM((2, 4, QTR, C), BF),
             pltpu.VMEM((T, C), BF),
-            dma((11,)), dma((2,)), dma((2,)), dma((7,)), dma((7,)), dma((3,)), dma((3,)),
+            pltpu.VMEM((2 * C, 128), BF),
+            pltpu.VMEM((128, C), BF),
+            dma((13,)), dma((2,)), dma((2,)), dma((7,)), dma((7,)), dma((3,)), dma((3,)),
             dma((13,)), dma((13,)), dma((6,)), dma((6,)), dma((8,)), dma((8,)), dma((8,)), dma((8,)),
             dma((6,)), dma((6,)), dma((6,)), dma((6,)),
         ],
@@ -498,6 +520,13 @@
         hsum,
         hexp,
     )
+    out, fresh = pl.pallas_call(
+        deliver,
+        out_shape=(jax.ShapeDtypeStruct((T, C), F32), jax.ShapeDtypeStruct((T, 2 * HC), BF)),
+        in_specs=[hbm] * 2,
+        out_specs=(hbm, hbm),
+        scratch_shapes=[pltpu.VMEM((T, C), F32), pltpu.VMEM((T, 2 * HC), BF), dma((4, PARTS))],
+    )(out, fresh)
     return out.reshape(1, 2, W, C), fresh.reshape(1, 2, W, 2 * HC)
 
 

time: 94.9 us -> 89.5 us (0.943)
  local copies, waits for them, and re-layouts: 4.13 us -> 0 us
  Pallas kernels: 89.9 us -> 88.5 us
    unnamed x2 -> x0, local copies, waits for them, and re-layouts: 4.13 us -> none
    pallas_call x1, Pallas kernels: 89.9 us -> 86.2 us  [shards(): pl.pallas_call(kernel, out_shape=(jax.ShapeDtypeStruct((T, C), F32), jax....]
    pallas_call x0 -> x1, Pallas kernels: none -> 2.32 us  [shards(): pl.pallas_call(deliver, out_shape=(jax.ShapeDtypeStruct((T, C), F32), jax...]
where the time goes in v3:
time: 89.5 us; the launch traced here: 89.3 us
  Pallas kernels  88.5 us (99%)
    pallas_call x1, Pallas kernels, shards(): pl.pallas_call(kernel, out_shape=(jax.ShapeDtypeStruct((T, C), F32), jax....  86.2 us
    pallas_call x1, Pallas kernels, shards(): pl.pallas_call(deliver, out_shape=(jax.ShapeDtypeStruct((T, C), F32), jax...  2.32 us

profile of v3, /device:TPU:1, one launch (start us, length us, event | category | flops | bytes accessed | tf_op | source)
XLA Modules:
  0.0 89.3 jit_solution(16349396467318121376)
XLA Ops:
  0.6 86.2 %shard_map.176 = (f32[384,640]{1,0:T(8,128)}, bf16[384,768]{1,0:T(8,128)(2,1)}) custom-call(bf16[384,640]{1,0:T(8,128)(2,1)} %bitcast.7, bf16[384,768]{1,0:T(8,128)(2,1)} %bitcast.6, bf16[3,1920,640]{2,1,0:T(8,128)(2,1)} %bitcast.5, bf16[640,384]{1,0:T(8,128)(2,1)} %wq_h.1, bf16[640,768]{1,0:T(8,128)(2,1)} %wkv_h.1, bf16[384,640]{1,0:T(8,128)(2,1)} %wout_h.1, ...), custom_call_target="tpu_custom_call" | custom-call | tf_op jit(solution)/shard_map/pallas_call | solution.py:463
  86.9 2.3 %shard_map.177 = (f32[384,640]{1,0:T(8,128)}, bf16[384,768]{1,0:T(8,128)(2,1)}) custom-call(f32[384,640]{1,0:T(8,128)} %get-tuple-element.6.out_in, bf16[384,768]{1,0:T(8,128)(2,1)} %get-tuple-element.7.fresh_in), custom_call_target="tpu_custom_call" | custom-call | tf_op jit(solution)/shard_map/pallas_call | solution.py:523

commit v4 on v3

--- a/solution.py
+++ b/solution.py
@@ -76,8 +76,7 @@
         pltpu.make_async_copy(hsum_h, hsum_ref, lsem.at[11]),
         pltpu.make_async_copy(hexp_h, hexp_ref, lsem.at[12]),
     ]
-    for c in loads:
-        c.start()
+    loads[0].start()
 
     barrier = pltpu.get_barrier_semaphore()
     greet = xy_peers + list(z_peers.values()) + [up, down] + list(f_peers.values())
@@ -128,6 +127,8 @@
     ]
     for c in wave1:
         c.start()
+    for c in loads[1:]:
+        c.start()
 
     for c in st1:
         c.wait_recv()
@@ -169,12 +170,14 @@
     hidden_row(lat[W : 2 * W], 2, None)
     loads[2].wait()
     cacc[...] = jnp.dot(hcat[W : W + T], convw[1], preferred_element_type=F32)
+    cacc[0:W] += jnp.dot(hcat[2 * W : 3 * W], convw[2], preferred_element_type=F32)
+    cacc[W:T] += jnp.dot(hcat[W : 2 * W], convw[0], preferred_element_type=F32)
     halos[0].wait_recv()
     halos[1].wait_recv()
     hidden_row(halo[0], 0, p > 0)
     hidden_row(halo[1], 3, p < 31)
-    cacc[...] += jnp.dot(hcat[0:T], convw[0], preferred_element_type=F32)
-    cacc[...] += jnp.dot(hcat[2 * W : 2 * W + T], convw[2], preferred_element_type=F32)
+    cacc[0:W] += jnp.dot(hcat[0:W], convw[0], preferred_element_type=F32)
+    cacc[W:T] += jnp.dot(hcat[3 * W : 4 * W], convw[2], preferred_element_type=F32)
     resid[...] = (lat[...].astype(F32) + cacc[...]).astype(BF)
 
     def half(h):

time: 89.5 us -> 89.5 us (level)
  no operation moved by 1% of the time
where the time goes in v4:
time: 89.5 us; the launch traced here: 89.3 us
  Pallas kernels  88.5 us (99%)
    pallas_call x1, Pallas kernels, shards(): pl.pallas_call(kernel, out_shape=(jax.ShapeDtypeStruct((T, C), F32), jax....  86.2 us
    pallas_call x1, Pallas kernels, shards(): pl.pallas_call(deliver, out_shape=(jax.ShapeDtypeStruct((T, C), F32), jax...  2.32 us

profile of v4, /device:TPU:1, one launch (start us, length us, event | category | flops | bytes accessed | tf_op | source)
XLA Modules:
  0.0 89.3 jit_solution(3102787326876647505)
XLA Ops:
  0.6 86.2 %shard_map.176 = (f32[384,640]{1,0:T(8,128)}, bf16[384,768]{1,0:T(8,128)(2,1)}) custom-call(bf16[384,640]{1,0:T(8,128)(2,1)} %bitcast.7, bf16[384,768]{1,0:T(8,128)(2,1)} %bitcast.6, bf16[3,1920,640]{2,1,0:T(8,128)(2,1)} %bitcast.5, bf16[640,384]{1,0:T(8,128)(2,1)} %wq_h.1, bf16[640,768]{1,0:T(8,128)(2,1)} %wkv_h.1, bf16[384,640]{1,0:T(8,128)(2,1)} %wout_h.1, ...), custom_call_target="tpu_custom_call" | custom-call | tf_op jit(solution)/shard_map/pallas_call | solution.py:466
  86.8 2.3 %shard_map.177 = (f32[384,640]{1,0:T(8,128)}, bf16[384,768]{1,0:T(8,128)(2,1)}) custom-call(f32[384,640]{1,0:T(8,128)} %get-tuple-element.6.out_in, bf16[384,768]{1,0:T(8,128)(2,1)} %get-tuple-element.7.fresh_in), custom_call_target="tpu_custom_call" | custom-call | tf_op jit(solution)/shard_map/pallas_call | solution.py:526
